TPU v7x, 32 devices: a whole 2x2x4 slice. The times are simulated.
32 devices in a mesh: dp: 16 (over z, y, x), tp: 2 (over core).
Axes of the slice: x: 2, y: 2, z: 4, core: 2. Of those that a mesh axis runs over, the one named last changes fastest.
Arguments:
- prefix_hidden: bfloat16 [1024, 7168], P('dp', 'tp'), may hold values from -6 to 6
- down_kv: bfloat16 [7168, 576], P('tp'), may hold values from -0.0625 to 0.0625
- latent_gain: float32 [512], replicated, may hold values from 0.1 to 1.9
- step_hidden: bfloat16 [128, 3, 7168], P('dp', None, 'tp'), may hold values from -6 to 6
- query_nope: bfloat16 [128, 3, 2048], P('dp', None, 'tp'), may hold values from -12 to 12
- query_rope: bfloat16 [128, 3, 1024], P('dp', None, 'tp'), may hold values from -120 to 120
- key_absorb: bfloat16 [16, 128, 512], P('tp'), may hold values from -0.5 to 0.5
- value_up: bfloat16 [16, 512, 128], P('tp'), may hold values from -0.25 to 0.25
- cache: bfloat16 [128, 128, 576], P('dp'), may hold values from -6 to 6
- cache_len: int32 [128], P('dp'), may hold values from 1 to 128, as said below
- counts: int32 [16], P('dp'), may hold values from 1 to 8, as said below
Outputs:
- attended: bfloat16 [128, 3, 2048], P('dp', None, 'tp')
Inputs may be any that keep to these rules, and one draw needn't show every extreme that they name: `cache_len`: each sample's cache holds valid rows first. `counts`: a replica's live samples are its first slots.
All inputs are finite; a program needn't handle non-finite values.
Results may differ from a plain program's by a relative error of at most 0.011.
Values may be sent and summed in bfloat16 or wider, within the bound.
A program may use at most 64 MiB of HBM per device.

v0:
```python
import jax
import jax.numpy as jnp
from jax import lax
from jax.sharding import PartitionSpec as P

PREFIX = 1024


def apply_rotary_embedding(values, positions):
    half_width = values.shape[-1] // 2
    frequencies = 10000.0 ** (-jnp.arange(half_width, dtype=jnp.float32) / half_width)
    angles = positions[..., None] * frequencies
    cosine = jnp.cos(angles)
    sine_part = jnp.sin(angles)
    first_half = values[..., :half_width]
    second_half = values[..., half_width:]
    return jnp.concatenate(
        [
            first_half * cosine - second_half * sine_part,
            first_half * sine_part + second_half * cosine,
        ],
        axis=-1,
    )


def finish(raw_rows, gain, positions):
    latent_width = gain.shape[0]
    latent = raw_rows[..., :latent_width]
    factor = lax.rsqrt(jnp.mean(latent * latent, axis=-1, keepdims=True) + 1e-06)
    normed = latent * factor * gain
    return jnp.concatenate(
        [normed, apply_rotary_embedding(raw_rows[..., latent_width:], positions)], axis=-1
    ).astype(jnp.bfloat16)


def own_keys(
    query_entries,
    key_entries,
    lengths,
    row_max,
    row_mass,
    row_total,
    attention_head_count,
    logit_scale,
    latent_width,
):
    total_keys = key_entries.shape[1]
    context = total_keys - query_entries.shape[1] // attention_head_count
    scores = (
        jnp.einsum("aru,aeu->are", query_entries, key_entries, preferred_element_type=jnp.float32)
        * logit_scale
    )
    key_ids = jnp.arange(total_keys, dtype=jnp.int32)
    row_step = jnp.arange(query_entries.shape[1], dtype=jnp.int32) // attention_head_count
    new_ok = (key_ids[None, :] >= context) & (key_ids[None, :] - context <= row_step[:, None])
    is_valid = (key_ids[None, None, :] < lengths[:, None, None]) | new_ok[None]
    new_max = jnp.maximum(
        row_max, jnp.max(jnp.where(is_valid, scores, -1e30), axis=2, keepdims=True)
    )
    weights = jnp.where(is_valid, jnp.exp(scores - new_max), 0.0)
    shrink = jnp.exp(row_max - new_max)
    row_mass = row_mass * shrink + jnp.sum(weights, axis=2, keepdims=True)
    row_total = row_total * shrink + jnp.einsum(
        "dev,dva->dea",
        weights,
        key_entries[..., :latent_width].astype(jnp.float32),
        precision=lax.Precision.HIGHEST,
    )
    return (row_total / row_mass).astype(jnp.bfloat16)


def local(
    prefix_hidden,
    down_kv,
    latent_gain,
    step_hidden,
    query_nope,
    query_rope,
    key_absorb,
    value_up,
    cache,
    cache_len,
    counts,
):
    key_width = down_kv.shape[1]
    latent_width = latent_gain.shape[0]
    slot_count, step_count, _ = step_hidden.shape
    attention_head_count, nope_width, _ = key_absorb.shape
    rope_width = key_width - latent_width
    logit_scale = (nope_width + rope_width) ** (-0.5)
    partial_rows = jnp.dot(prefix_hidden, down_kv, preferred_element_type=jnp.float32)
    step_part = jnp.dot(
        step_hidden.reshape(slot_count * step_count, -1),
        down_kv,
        preferred_element_type=jnp.float32,
    )
    step_unprojected = lax.psum(step_part, "tp").reshape(slot_count, step_count, key_width)
    step_ids = jnp.arange(step_count, dtype=jnp.int32)
    new_pos = (PREFIX + cache_len[:, None] + step_ids[None, :]).astype(jnp.float32)
    new_keys = finish(step_unprojected, latent_gain, new_pos)
    nope_rows = query_nope.reshape(slot_count, step_count, attention_head_count, nope_width)
    query_latent = jnp.einsum(
        "stha,hal->sthl", nope_rows, key_absorb, preferred_element_type=jnp.float32
    ).astype(jnp.bfloat16)
    query_rot = apply_rotary_embedding(
        query_rope.reshape(slot_count, step_count, attention_head_count, rope_width).astype(
            jnp.float32
        ),
        new_pos[:, :, None],
    ).astype(jnp.bfloat16)
    queries = jnp.concatenate([query_latent, query_rot], axis=-1).reshape(
        slot_count * step_count * attention_head_count, key_width
    )
    total_rows = queries.shape[0]
    block_rows = partial_rows.shape[0]
    common_prompt_rows = lax.psum_scatter(partial_rows, "tp", scatter_dimension=0, tiled=True)
    share_count = common_prompt_rows.shape[0]
    first_row = lax.axis_index("dp") * block_rows + lax.axis_index("tp") * share_count
    positions = (first_row + jnp.arange(share_count, dtype=jnp.int32)).astype(jnp.float32)
    prefix_keys = finish(common_prompt_rows, latent_gain, positions)
    key_piece = lax.all_gather(prefix_keys, ("dp", "tp"), axis=0, tiled=True)
    row_max = jnp.full((total_rows, 1), -1e30, jnp.float32)
    scores = (
        jnp.einsum("qc,kc->qk", queries, key_piece, preferred_element_type=jnp.float32)
        * logit_scale
    )
    new_max = jnp.maximum(row_max, jnp.max(scores, axis=1, keepdims=True))
    weights = jnp.exp(scores - new_max)
    row_mass = jnp.sum(weights, axis=1, keepdims=True)
    row_total = jnp.dot(
        weights, key_piece[:, :latent_width].astype(jnp.float32), precision=lax.Precision.HIGHEST
    )
    row_max, row_mass, row_total = (new_max, row_mass, row_total)
    per_slot = step_count * attention_head_count
    query_slots = queries.reshape(slot_count, per_slot, key_width)
    row_max = row_max.reshape(slot_count, per_slot, 1)
    row_mass = row_mass.reshape(slot_count, per_slot, 1)
    row_total = row_total.reshape(slot_count, per_slot, latent_width)
    key_entries = jnp.concatenate([cache, new_keys], axis=1)
    live_count = counts[0]
    is_live = jnp.arange(slot_count, dtype=jnp.int32) < live_count
    latent_out = own_keys(
        query_slots,
        key_entries,
        cache_len,
        row_max,
        row_mass,
        row_total,
        attention_head_count,
        logit_scale,
        latent_width,
    )
    latent_out = latent_out.reshape(slot_count, step_count, attention_head_count, latent_width)
    projected = jnp.einsum(
        "sthl,hlv->sthv", latent_out, value_up, preferred_element_type=jnp.float32
    )
    projected = jnp.where(is_live[:, None, None, None], projected, 0.0)
    return projected.reshape(slot_count, step_count, -1).astype(jnp.bfloat16)


def solution(mesh):
    in_specs = (
        P("dp", "tp"),
        P("tp", None),
        P(),
        P("dp", None, "tp"),
        P("dp", None, "tp"),
        P("dp", None, "tp"),
        P("tp", None, None),
        P("tp", None, None),
        P("dp", None, None),
        P("dp"),
        P("dp"),
    )
    out_specs = P("dp", None, "tp")
    return jax.shard_map(local, mesh=mesh, in_specs=in_specs, out_specs=out_specs, check_vma=False)
```

profile of v0, /device:TPU:1, one launch (start us, length us, event | category | flops | bytes accessed | tf_op | source)
XLA Modules:
  0.0 94.1 jit_solution(10727778882493169632)
XLA Ops:
  6.6 4.4 %fusion.45 = f32[64,576]{1,0:T(8,128)} fusion(bf16[64,3584]{1,0:T(8,128)(2,1)} %param.11, bf16[3584,576]{0,1:T(8,128)(2,1)} %param.12), kind=kOutput, calls=%fused_computation.84 | convolution fusion | flops 264241152 | bytes 4734976 | tf_op jit(solution)/shard_map/dot_general | solution.py:91
  11.8 0.1 reshape.260
  11.9 0.1 copy.33
  12.0 0.1 reshape.257
  12.2 3.3 %fusion.46 = f32[24,576]{1,0:T(8,128)S(1)} fusion(bf16[24,3584]{1,0:T(8,128)(2,1)S(1)} %reshape.257, bf16[3584,576]{0,1:T(8,128)(2,1)} %param.12), kind=kOutput, calls=%fused_computation.85 | convolution fusion | flops 99090432 | bytes 4356096 | tf_op jit(solution)/shard_map/dot_general | solution.py:92
  15.6 3.6 %psum.7 = f32[8,3,576]{2,0,1:T(8,128)S(1)} all-reduce(f32[8,3,576]{2,0,1:T(8,128)S(1)} %copy.34), channel_id=1, replica_groups=mesh['dp'=16,'tp'=2] {'tp'}, use_global_device_ids=true, to_apply=%region_3.0 | all-reduce | flops 13824 | bytes 110592 | tf_op jit(solution)/shard_map/psum | solution.py:97
  19.2 0.1 multiply_reduce_fusion.1
  19.3 1.8 %reduce-scatter.2.cloned.1.call-done = f32[32,576]{1,0:T(8,128)} async-done(((f32[64,576]{1,0:T(8,128)}), f32[32,576]{1,0:T(8,128)}) %reduce-scatter.2.cloned.1.call-update) | async-done | bytes 73744 | tf_op jit(solution)/shard_map/reduce_scatter | solution.py:116
  21.1 1.0 %multiply_reduce_fusion = f32[32]{0:T(128)S(1)} fusion(f32[32,576]{1,0:T(8,128)} %reduce-scatter.2.cloned.1.call-done), kind=kLoop, calls=%fused_computation.39 | loop fusion | flops 32736 | bytes 65664 | tf_op jit(solution)/shard_map/reduce_sum | solution.py:29
  22.1 0.9 multiply_convert_fusion
  23.0 0.9 fusion.36
  24.0 0.7 pad_maximum_fusion.1
  24.7 0.1 multiply_cosine_fusion.1
  24.8 0.1 pad_maximum_fusion.2
  24.9 0.6 copy.36
  25.5 0.1 fusion.43
  25.7 0.2 fusion.6
  25.9 0.1 pad_maximum_fusion
  26.1 0.7 copy-done.7
  26.8 0.7 copy.31
  27.5 0.7 copy.35
  28.4 2.6 %fusion.23 = (f32[8,24]{1,0:T(8,128)S(1)}, f32[8,24,131]{2,1,0:T(8,128)}) fusion(pred[24,131]{1,0:T(8,128)(4,1)S(1)} %compare_and_fusion, pred[8,131]{1,0:T(8,128)(4,1)S(1)} %iota_compare_fusion, bf16[8,3,576]{2,1,0:T(4,128)(2,1)} %copy.36, bf16[8,128,576]{2,1,0:T(8,128)(2,1)S(1)} %copy.35, bf16[8,3,8,576]{3,0,1,2:T(8,128)(2,1)} %copy-done.7), kind=kOutput, calls=%fused_computation.29 | convolution fusion | flops 31490112 | bytes 1534048 | tf_op jit(solution)/shard_map/aru,aeu->are/dot_general | solution.py:50
  31.0 49.4 %all-gather.2.cloned.1.call-done = bf16[1024,576]{1,0:T(8,128)(2,1)} async-done(((bf16[32,576]{1,0:T(8,128)(2,1)}), bf16[1024,576]{1,0:T(8,128)(2,1)}) %all-gather.2.cloned.1.call-update) | async-done | bytes 1179664 | tf_op jit(solution)/shard_map/all_gather | solution.py:121
  80.3 2.1 %fusion.44 = (f32[192]{0:T(256)S(1)}, f32[192,1024]{1,0:T(8,128)S(1)}) fusion(bf16[192,576]{1,0:T(8,128)(2,1)S(1)} %bitcast.41, bf16[1024,576]{1,0:T(8,128)(2,1)} %all-gather.2.cloned.1.call-done), kind=kOutput, calls=%fused_computation.83 | convolution fusion | flops 226885440 | bytes 2188032 | tf_op jit(solution)/shard_map/qc,kc->qk/dot_general | solution.py:124
  82.5 0.1 max_broadcast_in_dim.26
  82.5 0.3 fusion.20
  82.9 1.2 %fusion.25 = f32[8,24]{1,0:T(8,128)S(1)} fusion(f32[8,24,131]{2,1,0:T(8,128)} %get-tuple-element.22, f32[8,24]{1,0:T(8,128)S(1)} %max.14, pred[24,131]{1,0:T(8,128)(4,1)S(1)} %compare_and_fusion, pred[8,131]{1,0:T(8,128)(4,1)S(1)} %iota_compare_fusion), kind=kLoop, calls=%fused_computation.31 | loop fusion | flops 100416 | bytes 106336 | tf_op jit(solution)/shard_map/reduce_sum | solution.py:62
  84.2 0.8 fusion.16
  85.1 0.6 fusion.10
  85.7 0.6 copy-done.5
  86.3 0.3 fusion.12
  86.6 0.6 copy.59
  (52 shorter events, 0.7 us)
Async XLA Ops:
  6.5 19.1 %copy-start = (bf16[8,128,512]{2,1,0:T(8,128)(2,1)S(1)}, bf16[8,128,512]{2,1,0:T(8,128)(2,1)}, u32[]{:S(2)}) copy-start(bf16[8,128,512]{2,1,0:T(8,128)(2,1)} %param.17) | copy-start | bytes 3145732
  6.5 5.2 %copy-start.13 = (s32[8]{0:T(128)S(1)}, s32[8]{0:T(128)}, u32[]{:S(2)}) copy-start(s32[8]{0:T(128)} %param.20) | copy-start | bytes 100
  6.5 5.2 %copy-start.11 = (bf16[8,3,512]{2,0,1:T(8,128)(2,1)S(1)}, bf16[8,3,512]{2,0,1:T(8,128)(2,1)}, u32[]{:S(2)}) copy-start(bf16[8,3,512]{2,0,1:T(8,128)(2,1)} %param.16) | copy-start | bytes 73732
  6.5 5.3 %copy-start.9 = (bf16[8,3,3584]{2,0,1:T(8,128)(2,1)S(1)}, bf16[8,3,3584]{2,0,1:T(8,128)(2,1)}, u32[]{:S(2)}) copy-start(bf16[8,3,3584]{2,0,1:T(8,128)(2,1)} %param.14) | copy-start | bytes 516100
  6.5 14.6 %reduce-scatter.2.cloned.1.call-start = ((), (), s32[]{:S(2)}) async-start(), calls=%async_computation.1 | async-start | bytes 245760 | tf_op jit(solution)/shard_map/reduce_scatter | solution.py:116
  11.0 69.3 %all-gather.2.cloned.1.call-start = ((), (), s32[]{:S(2)}) async-start(), calls=%async_computation.2 | async-start | bytes 1351680 | tf_op jit(solution)/shard_map/all_gather | solution.py:121
  12.1 7.1 %copy-start.12 = (f32[512]{0:T(512)S(1)}, f32[512]{0:T(512)}, u32[]{:S(2)}) copy-start(f32[512]{0:T(512)} %param.13) | copy-start | bytes 6148
  15.5 10.2 %copy-start.14 = (bf16[8,3,1024]{2,0,1:T(8,128)(2,1)S(1)}, bf16[8,3,1024]{2,0,1:T(8,128)(2,1)}, u32[]{:S(2)}) copy-start(bf16[8,3,1024]{2,0,1:T(8,128)(2,1)} %param.15) | copy-start | bytes 147460
  25.6 1.9 %copy-start.4 = (bf16[8,128,576]{1,2,0:T(8,128)(2,1)S(1)}, bf16[8,128,576]{1,2,0:T(8,128)(2,1)}, u32[]{:S(2)}) copy-start(bf16[8,128,576]{1,2,0:T(8,128)(2,1)} %param.19) | copy-start | bytes 3538948
  26.0 0.7 copy-start.7
  28.2 52.1 %copy-start.2 = (bf16[8,128,576]{2,1,0:T(8,128)(2,1)}, bf16[8,128,576]{2,1,0:T(8,128)(2,1)S(1)}, u32[]{:S(2)}) copy-start(bf16[8,128,576]{2,1,0:T(8,128)(2,1)S(1)} %copy.35) | copy-start | bytes 3538948
  28.2 52.1 %copy-start.6 = (bf16[8,3,8,576]{3,2,1,0:T(8,128)(2,1)S(1)}, bf16[8,3,8,576]{3,2,1,0:T(8,128)(2,1)}, u32[]{:S(2)}) copy-start(bf16[8,3,8,576]{3,2,1,0:T(8,128)(2,1)} %copy.31) | copy-start | bytes 663556
  80.3 3.8 %copy-start.1 = (bf16[1024,576]{1,0:T(8,128)(2,1)S(1)}, bf16[1024,576]{1,0:T(8,128)(2,1)}, u32[]{:S(2)}) copy-start(bf16[1024,576]{1,0:T(8,128)(2,1)} %all-gather.2.cloned.1.call-done) | copy-start | bytes 3538948
  82.8 2.2 %copy-start.8 = (f32[8,24,131]{2,1,0:T(8,128)S(1)}, f32[8,24,131]{2,1,0:T(8,128)}, u32[]{:S(2)}) copy-start(f32[8,24,131]{2,1,0:T(8,128)} %get-tuple-element.22) | copy-start | bytes 301828
  82.8 2.2 %copy-start.10 = (bf16[8,3,576]{2,1,0:T(4,128)(2,1)S(1)}, bf16[8,3,576]{2,1,0:T(4,128)(2,1)}, u32[]{:S(2)}) copy-start(bf16[8,3,576]{2,1,0:T(4,128)(2,1)} %copy.36) | copy-start | bytes 82948
  82.9 2.1 %copy-start.3 = (bf16[8,128,576]{2,1,0:T(8,128)(2,1)S(1)}, bf16[8,128,576]{2,1,0:T(8,128)(2,1)}, u32[]{:S(2)}) copy-start(bf16[8,128,576]{2,1,0:T(8,128)(2,1)} %copy-done.2) | copy-start | bytes 3538948
  85.1 1.2 %copy-start.5 = (bf16[8,512,128]{2,1,0:T(8,128)(2,1)S(1)}, bf16[8,512,128]{2,1,0:T(8,128)(2,1)}, u32[]{:S(2)}) copy-start(bf16[8,512,128]{2,1,0:T(8,128)(2,1)} %param.18) | copy-start | bytes 3145732
Sparse Core Ops, SparseCore 0:
  11.1 9.9 reduce-scatter.1
  24.8 55.4 all-gather.1
where the time goes:
time: 94.7 us; the launch traced here: 94.1 us
  waiting for transfers between devices  51.2 us (54%)
  matrix products  14.4 us (15%)
  between operations  14.4 us (15%)
  other arithmetic  5.73 us (6%)
  local copies, waits for them, and re-layouts  4.68 us (5%)
  blocking collectives  3.58 us (4%)
    all_gather x1, waiting for transfers between devices, local(): key_piece = lax.all_gather(prefix_keys, ('dp', 'tp'), axis=0, tiled=True)  49.4 us
    dot_general x1, matrix products, local(): jnp.dot(prefix_hidden, down_kv, preferred_element_type=jnp.float32)  4.39 us
    psum x1, blocking collectives, local(): lax.psum(step_part, 'tp').reshape(slot_count, step_count, key_width)  3.58 us
    dot_general x1, matrix products, local(): jnp.dot(step_hidden.reshape(slot_count * step_count, -1), down_kv, prefer...  3.34 us
    dot_general x1, matrix products, own_keys(): jnp.einsum('aru,aeu->are', query_entries, key_entries, preferred_element_...  2.56 us
    unnamed x32, local copies, waits for them, and re-layouts  2.16 us
    dot_general x1, matrix products, local(): jnp.einsum('qc,kc->qk', queries, key_piece, preferred_element_type=jnp.fl...  2.12 us
    another operation x4, other arithmetic  1.97 us
  transfers between devices with their start and end apart: 2, of which 2 were waited for; matrix products, arithmetic and copies ran while one was open for 10% of the time, Pallas kernels for 0%

commit v1 on v0

--- a/solution.py
+++ b/solution.py
@@ -1,9 +1,16 @@
+import functools
+
 import jax
 import jax.numpy as jnp
 from jax import lax
+from jax.experimental import pallas as pl
+from jax.experimental.pallas import tpu as pltpu
 from jax.sharding import PartitionSpec as P
 
 PREFIX = 1024
+MESH = pl.DeviceIdType.MESH
+NEG = -1e30
+LOG2E = 1.4426950408889634
 
 
 def apply_rotary_embedding(values, positions):
@@ -158,6 +165,359 @@
     return projected.reshape(slot_count, step_count, -1).astype(jnp.bfloat16)
 
 
+def rotate(x, cosine, signed_sine):
+    lane = lax.broadcasted_iota(jnp.int32, x.shape, 1) % 64
+    swapped = jnp.where(lane < 32, pltpu.roll(x, 96, 1), pltpu.roll(x, 32, 1))
+    return x * cosine + swapped * signed_sine
+
+
+def fused_kernel(
+    prefix_hbm,
+    step_hbm,
+    down_hbm,
+    nope_ref,
+    rope_ref,
+    absorb_hbm,
+    value_hbm,
+    cache_hbm,
+    gain_ref,
+    cos_ref,
+    sin_ref,
+    bias_ref,
+    out_ref,
+    hidden,
+    down,
+    absorb,
+    value,
+    own,
+    keys,
+    queries,
+    partial,
+    arrived,
+    load_sem,
+    pair_send,
+    pair_recv,
+    send_sem,
+    z_recv,
+    x_recv,
+    y_recv,
+    d1_recv,
+    d2_recv,
+    s_recv,
+    *,
+    chunks,
+    logit_scale,
+):
+    dp = lax.axis_index("dp")
+    tp = lax.axis_index("tp")
+    z, y, x = dp // 4, (dp // 2) % 2, dp % 2
+    latent = gain_ref.shape[1]
+    width = keys.shape[1]
+    heads = absorb.shape[0]
+    nope = absorb.shape[1]
+    share = 32
+    rows = 32
+
+    def place(zz, yy, xx):
+        return zz * 4 + yy * 2 + xx
+
+    def zof(shift):
+        return lax.rem(z + shift + 4, 4)
+
+    x_dev = (place(z, y, 1 - x), tp)
+    y_dev = (place(z, 1 - y, x), tp)
+    sib_dev = (dp, 1 - tp)
+    z_devs = {d: (place(zof(d), y, x), tp) for d in (1, 2, 3)}
+
+    barrier = pltpu.get_barrier_semaphore()
+    for dev in (x_dev, y_dev, sib_dev, z_devs[1], z_devs[2], z_devs[3]):
+        pl.semaphore_signal(barrier, inc=1, device_id=dev, device_id_type=MESH)
+
+    prefix_rows = prefix_hbm.shape[0]
+    depth = down_hbm.shape[0] // chunks
+    loads = []
+
+    def load(src, dst, i):
+        copy = pltpu.make_async_copy(src, dst, load_sem.at[i])
+        copy.start()
+        return copy
+
+    hid_a = load(prefix_hbm, hidden.at[pl.ds(0, prefix_rows), :], 0)
+    hid_b = load(step_hbm, hidden.at[pl.ds(prefix_rows, rows), :], 1)
+    for i in range(chunks):
+        span = pl.ds(i * depth, depth)
+        loads.append(load(down_hbm.at[span, :], down.at[span, :], 2 + i))
+    ab_load = load(absorb_hbm, absorb, 2 + chunks)
+    ca_load = load(cache_hbm, own.at[pl.ds(0, cache_hbm.shape[0]), :], 3 + chunks)
+    va_load = load(value_hbm, value, 4 + chunks)
+
+    hid_a.wait()
+    hid_b.wait()
+    total = None
+    for i in range(chunks):
+        loads[i].wait()
+        part = jnp.dot(
+            hidden[:, i * depth : (i + 1) * depth],
+            down[i * depth : (i + 1) * depth, :],
+            preferred_element_type=jnp.float32,
+        )
+        total = part if total is None else total + part
+    partial[...] = total
+
+    pl.semaphore_wait(barrier, 6)
+    theirs = pl.ds(pl.multiple_of((1 - tp) * share, share), share)
+    mine = pl.ds(pl.multiple_of(tp * share, share), share)
+
+    def remote(src, dst, ssem, rsem, dev):
+        return pltpu.make_async_remote_copy(
+            src_ref=src, dst_ref=dst, send_sem=ssem, recv_sem=rsem, device_id=dev, device_id_type=MESH
+        )
+
+    pair_a = remote(
+        partial.at[theirs, :], arrived.at[pl.ds(0, share), :], pair_send.at[0], pair_recv.at[0], sib_dev
+    )
+    pair_b = remote(
+        partial.at[pl.ds(prefix_rows, rows), :],
+        arrived.at[pl.ds(share, rows), :],
+        pair_send.at[1],
+        pair_recv.at[1],
+        sib_dev,
+    )
+    pair_a.start()
+    pair_b.start()
+
+    def finished(raw, at):
+        low = raw[:, :latent]
+        factor = lax.rsqrt(jnp.mean(low * low, axis=1, keepdims=True) + 1e-06)
+        rope = raw[:, latent:]
+        both = jnp.concatenate([rope, rope], axis=1)
+        turned = rotate(both, cos_ref[at : at + rows, :], sin_ref[at : at + rows, :])
+        return (low * factor * gain_ref[...]).astype(jnp.bfloat16), turned[:, : width - latent].astype(
+            jnp.bfloat16
+        )
+
+    pair_a.wait_recv()
+    low, high = finished(partial[mine, :] + arrived[0:share, :], 0)
+
+    def block(core, zz, yy, xx):
+        return pl.multiple_of((core * 16 + place(zz, yy, xx)) * share, share)
+
+    my_block = pl.ds(block(tp, z, y, x), share)
+    keys[my_block, :latent] = low
+    keys[my_block, latent:] = high
+
+    sends = []
+
+    def send(start, size, rsem, dev):
+        ref = keys.at[pl.ds(start, size), :]
+        copy = remote(ref, ref, send_sem.at[len(sends)], rsem, dev)
+        copy.start()
+        sends.append(copy)
+
+    def await_block(start, size, rsem, dev):
+        ref = keys.at[pl.ds(start, size), :]
+        remote(ref, ref, send_sem.at[0], rsem, dev).wait_recv()
+
+    start = block(tp, z, y, x)
+    for d in (2, 1, 3):
+        send(start, share, z_recv.at[d], z_devs[d])
+    send(start, share, x_recv.at[0], x_dev)
+    send(start, share, y_recv.at[0], y_dev)
+    send(start, share, s_recv.at[0], sib_dev)
+
+    ab_load.wait()
+    for h in range(heads):
+        ql = jnp.dot(
+            nope_ref[:, h * nope : (h + 1) * nope], absorb[h], preferred_element_type=jnp.float32
+        )
+        queries[h * rows : (h + 1) * rows, :latent] = ql.astype(jnp.bfloat16)
+    for p in range(heads // 2):
+        turned = rotate(
+            rope_ref[:, p * 128 : (p + 1) * 128].astype(jnp.float32),
+            cos_ref[rows : 2 * rows, :],
+            sin_ref[rows : 2 * rows, :],
+        ).astype(jnp.bfloat16)
+        queries[2 * p * rows : (2 * p + 1) * rows, latent:] = turned[:, :64]
+        queries[(2 * p + 1) * rows : (2 * p + 2) * rows, latent:] = turned[:, 64:]
+
+    for d in (1, 3, 2):
+        zs = zof(-d)
+        start = block(tp, zs, y, x)
+        await_block(start, share, z_recv.at[d], z_devs[d])
+        send(start, share, x_recv.at[d], x_dev)
+        send(start, share, y_recv.at[d], y_dev)
+        send(start, share, s_recv.at[d], sib_dev)
+
+    def forward(d):
+        zs = zof(-d)
+        start = block(tp, zs, y, 1 - x)
+        await_block(start, share, x_recv.at[d], x_dev)
+        send(start, share // 2, d1_recv.at[d], y_dev)
+        send(start, share, s_recv.at[4 + d], sib_dev)
+        start = block(tp, zs, 1 - y, x)
+        await_block(start, share, y_recv.at[d], y_dev)
+        send(start + share // 2, share // 2, d2_recv.at[d], x_dev)
+        send(start, share, s_recv.at[8 + d], sib_dev)
+
+    forward(0)
+
+    ctx = cache_hbm.shape[0]
+    pair_b.wait_recv()
+    low, high = finished(partial[prefix_rows:, :] + arrived[share:, :], rows)
+    own[ctx : ctx + rows, :latent] = low
+    own[ctx : ctx + rows, latent:] = high
+    own[ctx + rows :, :] = jnp.zeros((own.shape[0] - ctx - rows, width), jnp.bfloat16)
+    ca_load.wait()
+    q = queries[...]
+    factor = logit_scale * LOG2E
+    nt = (((1,), (1,)), ((), ()))
+    s_own = lax.dot_general(q, own[...], nt, preferred_element_type=jnp.float32)
+    s_own = (s_own.reshape(heads, rows, -1) + bias_ref[...][None]).reshape(heads * rows, -1)
+    m_own = jnp.max(s_own, axis=1, keepdims=True)
+
+    for d in (1, 3, 2):
+        forward(d)
+
+    p_own = jnp.exp2((s_own - m_own) * factor)
+    l_own = jnp.sum(p_own, axis=1, keepdims=True)
+    o_own = jnp.dot(
+        p_own.astype(jnp.bfloat16), own[:, :latent], preferred_element_type=jnp.float32
+    )
+
+    for d in (0, 1, 3, 2):
+        start = block(tp, zof(-d), 1 - y, 1 - x)
+        await_block(start, share // 2, d1_recv.at[d], y_dev)
+        await_block(start + share // 2, share // 2, d2_recv.at[d], x_dev)
+        send(start, share, s_recv.at[12 + d], sib_dev)
+
+    for d in (0, 1, 3, 2):
+        zs = zof(-d)
+        await_block(block(1 - tp, zs, y, x), share, s_recv.at[d], sib_dev)
+        await_block(block(1 - tp, zs, y, 1 - x), share, s_recv.at[4 + d], sib_dev)
+        await_block(block(1 - tp, zs, 1 - y, x), share, s_recv.at[8 + d], sib_dev)
+        await_block(block(1 - tp, zs, 1 - y, 1 - x), share, s_recv.at[12 + d], sib_dev)
+
+    va_load.wait()
+    s_all = lax.dot_general(q, keys[...], nt, preferred_element_type=jnp.float32)
+    m_all = jnp.maximum(m_own, jnp.max(s_all, axis=1, keepdims=True))
+    p_all = jnp.exp2((s_all - m_all) * factor)
+    shrink = jnp.exp2((m_own - m_all) * factor)
+    mass = jnp.sum(p_all, axis=1, keepdims=True) + l_own * shrink
+    mixed = jnp.dot(p_all.astype(jnp.bfloat16), keys[:, :latent], preferred_element_type=jnp.float32)
+    mixed = ((mixed + o_own * shrink) / mass).astype(jnp.bfloat16)
+    vdim = value.shape[2]
+    for h in range(heads):
+        out_ref[:, h * vdim : (h + 1) * vdim] = jnp.dot(
+            mixed[h * rows : (h + 1) * rows, :], value[h], preferred_element_type=jnp.float32
+        ).astype(jnp.bfloat16)
+
+    pair_a.wait_send()
+    pair_b.wait_send()
+    for copy in sends:
+        copy.wait_send()
+
+
+def local_fused(
+    prefix_hidden,
+    down_kv,
+    latent_gain,
+    step_hidden,
+    query_nope,
+    query_rope,
+    key_absorb,
+    value_up,
+    cache,
+    cache_len,
+    counts,
+):
+    key_width = down_kv.shape[1]
+    latent_width = latent_gain.shape[0]
+    slots, steps, _ = step_hidden.shape
+    heads, nope_width, _ = key_absorb.shape
+    vdim = value_up.shape[2]
+    rope_width = key_width - latent_width
+    logit_scale = (nope_width + rope_width) ** (-0.5)
+    context = cache.shape[1]
+    rows = slots * 4
+    own_rows = slots * context + 128
+    block_rows = prefix_hidden.shape[0]
+    share = block_rows // 2
+
+    def four(values):
+        return jnp.pad(values, ((0, 0), (0, 4 - steps), (0, 0))).reshape(rows, -1)
+
+    first = lax.axis_index("dp") * block_rows + lax.axis_index("tp") * share
+    step_ids = jnp.arange(4, dtype=jnp.int32)
+    new_pos = (PREFIX + cache_len[:, None] + step_ids[None, :]).reshape(rows)
+    positions = jnp.concatenate([first + jnp.arange(share, dtype=jnp.int32), new_pos])
+    lane = jnp.arange(128, dtype=jnp.int32)
+    half = rope_width // 2
+    frequencies = 10000.0 ** (-(lane % half).astype(jnp.float32) / half)
+    angles = positions.astype(jnp.float32)[:, None] * frequencies[None, :]
+    cosine = jnp.cos(angles)
+    signed_sine = jnp.where(lane[None, :] % rope_width < half, -1.0, 1.0) * jnp.sin(angles)
+
+    row = jnp.arange(rows, dtype=jnp.int32)[:, None]
+    col = jnp.arange(own_rows, dtype=jnp.int32)[None, :]
+    limit = jnp.repeat(cache_len, 4)[:, None]
+    in_cache = (col < slots * context) & (col // context == row // 4) & (col % context < limit)
+    fresh = col - slots * context
+    in_new = (fresh >= 0) & (fresh // 4 == row // 4) & (fresh % 4 <= row % 4)
+    bias = jnp.where(in_cache | in_new, 0.0, NEG)
+
+    chunks = 7
+    vmem = pl.BlockSpec(memory_space=pltpu.VMEM)
+    anyw = pl.BlockSpec(memory_space=pl.ANY)
+    dma = pltpu.SemaphoreType.DMA
+    bf = jnp.bfloat16
+    out = pl.pallas_call(
+        functools.partial(fused_kernel, chunks=chunks, logit_scale=logit_scale),
+        out_shape=jax.ShapeDtypeStruct((rows, heads * vdim), bf),
+        in_specs=[anyw, anyw, anyw, vmem, vmem, anyw, anyw, anyw, vmem, vmem, vmem, vmem],
+        out_specs=vmem,
+        scratch_shapes=[
+            pltpu.VMEM((block_rows + rows, prefix_hidden.shape[1]), bf),
+            pltpu.VMEM(down_kv.shape, bf),
+            pltpu.VMEM(key_absorb.shape, bf),
+            pltpu.VMEM(value_up.shape, bf),
+            pltpu.VMEM((own_rows, key_width), bf),
+            pltpu.VMEM((PREFIX, key_width), bf),
+            pltpu.VMEM((heads * rows, key_width), bf),
+            pltpu.VMEM((block_rows + rows, key_width), jnp.float32),
+            pltpu.VMEM((share + rows, key_width), jnp.float32),
+            dma((5 + chunks,)),
+            dma((2,)),
+            dma((2,)),
+            dma((40,)),
+            dma((4,)),
+            dma((4,)),
+            dma((4,)),
+            dma((4,)),
+            dma((4,)),
+            dma((16,)),
+        ],
+        compiler_params=pltpu.CompilerParams(
+            collective_id=0, has_side_effects=True, vmem_limit_bytes=48 * 1024 * 1024
+        ),
+    )(
+        prefix_hidden,
+        four(step_hidden),
+        down_kv,
+        four(query_nope),
+        four(query_rope),
+        key_absorb,
+        value_up,
+        cache.reshape(slots * context, key_width),
+        latent_gain[None, :],
+        cosine,
+        signed_sine,
+        bias,
+    )
+    is_live = jnp.arange(slots, dtype=jnp.int32) < counts[0]
+    out = out.reshape(slots, 4, heads * vdim)[:, :steps]
+    return jnp.where(is_live[:, None, None], out, jnp.zeros((), bf))
+
+
 def solution(mesh):
     in_specs = (
         P("dp", "tp"),
@@ -173,4 +533,5 @@
         P("dp"),
     )
     out_specs = P("dp", None, "tp")
-    return jax.shard_map(local, mesh=mesh, in_specs=in_specs, out_specs=out_specs, check_vma=False)
+    fused = mesh.shape["dp"] == 16 and mesh.shape["tp"] == 2
+    return jax.shard_map(local_fused if fused else local, mesh=mesh, in_specs=in_specs, out_specs=out_specs, check_vma=False)

time: 94.7 us -> 43.4 us (0.46)
  waiting for transfers between devices: 51.2 us -> 0 us
  Pallas kernels: 0 us -> 24.5 us
  matrix products: 14.4 us -> 0 us
  between operations: 14.4 us -> 0.83 us
  local copies, waits for them, and re-layouts: 4.68 us -> 15.6 us
  other arithmetic: 5.73 us -> 1.88 us
  blocking collectives: 3.58 us -> 0 us
    all_gather x1 -> x0, waiting for transfers between devices: 49.4 us -> none  [local(): key_piece = lax.all_gather(prefix_keys, ('dp', 'tp'), axis=0, tiled=True)]
    pallas_call x0 -> x1, Pallas kernels: none -> 24.5 us  [local_fused(): pl.pallas_call(functools.partial(fused_kernel, chunks=chunks, logit_scale...]
    dot_general x8 -> x0, matrix products: 14.4 us -> none  [the longest x1 4.39 us: local(): jnp.dot(prefix_hidden, down_kv, preferred_element_type=jnp.float32)]
    unnamed x32 -> x27, local copies, waits for them, and re-layouts: 2.16 us -> 13.7 us
    psum x1 -> x0, blocking collectives: 3.58 us -> none  [local(): lax.psum(step_part, 'tp').reshape(slot_count, step_count, key_width)]
    reduce_sum x4 -> x0, other arithmetic: 2.54 us -> none  [the longest x1 1.21 us: own_keys(): row_mass = row_mass * shrink + jnp.sum(weights, axis=2, keepdims=True)]
    another operation x5 -> x0, other arithmetic: 1.98 us -> none
    reduce_scatter x1 -> x0, waiting for transfers between devices: 1.8 us -> none  [local(): lax.psum_scatter(partial_rows, 'tp', scatter_dimension=0, tiled=True)]
  transfers between devices with their start and end apart: 2 -> 0, of which waited for: 2 -> 0; matrix products, arithmetic and copies ran while one was open for 10% -> 0% of each run, Pallas kernels for 0% -> 0%
where the time goes in v1:
time: 43.4 us; the launch traced here: 42.8 us
  Pallas kernels  24.5 us (56%)
  local copies, waits for them, and re-layouts  15.6 us (36%)
  other arithmetic  1.88 us (4%)
  between operations  0.83 us (2%)
    pallas_call x1, Pallas kernels, local_fused(): pl.pallas_call(functools.partial(fused_kernel, chunks=chunks, logit_scale...  24.5 us
    unnamed x27, local copies, waits for them, and re-layouts  13.7 us
    reshape x3, local copies, waits for them, and re-layouts, four(): return jnp.pad(values, ((0, 0), (0, 4 - steps), (0, 0))).reshape(rows, -1)  1.43 us

profile of v1, /device:TPU:1, one launch (start us, length us, event | category | flops | bytes accessed | tf_op | source)
XLA Modules:
  0.0 42.8 jit_solution(610456678331294354)
XLA Ops:
  0.0 1.0 %copy.25 = bf16[8,3,3584]{2,1,0:T(4,128)(2,1)S(1)} copy(bf16[8,3,3584]{2,0,1:T(8,128)(2,1)} %param.14) | data formatting | bytes 344064
  1.0 0.1 pad.12.clone
  1.1 0.8 %reshape.242.step_hbm = bf16[32,3584]{1,0:T(8,128)(2,1)} reshape(bf16[8,4,3584]{2,1,0:T(4,128)(2,1)S(1)} %pad.12.clone) | data formatting | bytes 458752 | tf_op jit(solution)/shard_map/reshape | solution.py:447
  1.9 0.0 copy-start.8
  1.9 0.0 copy-start.9
  1.9 0.0 copy-start.10
  1.9 0.0 copy-start.1
  1.9 0.0 copy-start.7
  2.0 6.7 %copy.22.down_hbm = bf16[3584,576]{1,0:T(8,128)(2,1)} copy(bf16[3584,576]{0,1:T(8,128)(2,1)} %param.12) | data formatting | bytes 8257536 | tf_op args[1]
  8.7 0.0 copy-done.8
  8.8 0.0 copy-done.9
  8.8 0.6 %reshape.244.rope_ref = bf16[32,512]{1,0:T(8,128)(2,1)} reshape(bf16[8,4,512]{2,1,0:T(4,128)(2,1)S(1)} %pad.14.clone) | data formatting | bytes 65536 | tf_op jit(solution)/shard_map/reshape | solution.py:447
  9.5 1.7 %copy.21 = bf16[8,128,576]{2,1,0:T(8,128)(2,1)S(1)} copy(bf16[8,128,576]{1,2,0:T(8,128)(2,1)} %param.19) | data formatting | bytes 2359296 | tf_op args[8]
  11.2 0.0 copy-done.10
  11.2 0.1 iota_add_fusion.1
  11.3 0.1 add.129
  11.4 0.1 add_convert_fusion
  11.4 0.8 %fusion = (f32[64,128]{1,0:T(8,128)}, f32[64,128]{1,0:T(8,128)}) fusion(f32[128]{0:T(128)S(1)} %get-tuple-element.7, f32[128]{0:T(128)S(1)} %get-tuple-element.8, f32[64]{0:T(128)S(1)} %add_convert_fusion), kind=kLoop, calls=%fused_computation.4 | loop fusion | flops 16384 | bytes 66816 | tf_op jit(solution)/shard_map/mul | solution.py:458
  12.3 0.1 broadcast_in_dim.46
  12.4 0.1 lt.78
  12.5 0.1 or_select_fusion.bias_ref
  12.6 0.0 copy-done
  12.6 0.0 copy-done.1
  12.6 0.0 copy-done.7
  12.7 0.0 copy-start.2
  12.7 0.9 %copy-done.2 = bf16[32,3584]{1,0:T(8,128)(2,1)S(1)} copy-done((bf16[32,3584]{1,0:T(8,128)(2,1)S(1)}, bf16[32,3584]{1,0:T(8,128)(2,1)}, u32[]{:S(2)}) %copy-start.2) | copy-done | bytes 229400
  13.6 1.0 %copy-done.3 = bf16[64,3584]{1,0:T(8,128)(2,1)S(1)} copy-done((bf16[64,3584]{1,0:T(8,128)(2,1)S(1)}, bf16[64,3584]{1,0:T(8,128)(2,1)}, u32[]{:S(2)}) %copy-start.3) | copy-done | bytes 458776
  14.6 0.8 %copy-done.4 = bf16[32,512]{1,0:T(8,128)(2,1)S(1)} copy-done((bf16[32,512]{1,0:T(8,128)(2,1)S(1)}, bf16[32,512]{1,0:T(8,128)(2,1)}, u32[]{:S(2)}) %copy-start.4) | copy-done | bytes 32792
  15.4 0.8 %copy-done.5 = f32[64,128]{1,0:T(8,128)S(1)} copy-done((f32[64,128]{1,0:T(8,128)S(1)}, f32[64,128]{1,0:T(8,128)}, u32[]{:S(2)}) %copy-start.5) | copy-done | bytes 32792
  16.1 0.8 %copy-done.6 = f32[64,128]{1,0:T(8,128)S(1)} copy-done((f32[64,128]{1,0:T(8,128)S(1)}, f32[64,128]{1,0:T(8,128)}, u32[]{:S(2)}) %copy-start.6) | copy-done | bytes 32792
  16.9 24.5 %shard_map.109 = bf16[32,1024]{1,0:T(8,128)(2,1)S(1)} custom-call(bf16[64,3584]{1,0:T(8,128)(2,1)S(1)} %copy-done.3, bf16[32,3584]{1,0:T(8,128)(2,1)S(1)} %copy-done.2, bf16[3584,576]{1,0:T(8,128)(2,1)} %copy.22.down_hbm, bf16[32,1024]{1,0:T(8,128)(2,1)S(1)} %reshape.243.nope_ref, bf16[32,512]{1,0:T(8,128)(2,1)S(1)} %copy-done.4, ...), custom_call_target="tpu_custom_call" | custom-call | tf_op jit(solution)/shard_map/pallas_call | solution.py:473
  42.1 0.7 %copy_select_fusion = bf16[8,3,1024]{2,0,1:T(8,128)(2,1)} fusion(bf16[8,3,1024]{2,1,0:T(4,128)(2,1)S(1)} %bitcast.7, pred[8]{0:T(512)(128)(4,1)S(1)} %iota_compare_fusion.1), kind=kLoop, calls=%fused_computation.1 | loop fusion | flops 24576 | bytes 98312 | tf_op jit(solution)/shard_map/jit(_where)/select_n | solution.py:518
  (19 shorter events, 0.2 us)
Async XLA Ops:
  1.9 6.7 %copy-start.8 = (bf16[8,3,1024]{2,0,1:T(8,128)(2,1)S(1)}, bf16[8,3,1024]{2,0,1:T(8,128)(2,1)}, u32[]{:S(2)}) copy-start(bf16[8,3,1024]{2,0,1:T(8,128)(2,1)} %param.15) | copy-start | bytes 147460
  1.9 6.9 %copy-start.9 = (bf16[8,3,512]{2,0,1:T(8,128)(2,1)S(1)}, bf16[8,3,512]{2,0,1:T(8,128)(2,1)}, u32[]{:S(2)}) copy-start(bf16[8,3,512]{2,0,1:T(8,128)(2,1)} %param.16) | copy-start | bytes 73732
  1.9 9.3 %copy-start.10 = (s32[8]{0:T(128)S(1)}, s32[8]{0:T(128)}, u32[]{:S(2)}) copy-start(s32[8]{0:T(128)} %param.20) | copy-start | bytes 100
  1.9 10.7 %copy-start = (bf16[8,128,512]{2,1,0:T(8,128)(2,1)S(1)}, bf16[8,128,512]{2,1,0:T(8,128)(2,1)}, u32[]{:S(2)}) copy-start(bf16[8,128,512]{2,1,0:T(8,128)(2,1)} %absorb_hbm.1) | copy-start | bytes 3145732
  1.9 10.7 %copy-start.1 = (bf16[8,512,128]{2,1,0:T(8,128)(2,1)S(1)}, bf16[8,512,128]{2,1,0:T(8,128)(2,1)}, u32[]{:S(2)}) copy-start(bf16[8,512,128]{2,1,0:T(8,128)(2,1)} %value_hbm.1) | copy-start | bytes 3145732
  1.9 10.7 %copy-start.7 = (f32[512]{0:T(512)S(1)}, f32[512]{0:T(512)}, u32[]{:S(2)}) copy-start(f32[512]{0:T(512)} %param.13) | copy-start | bytes 6148
  12.7 0.9 %copy-start.2 = (bf16[32,3584]{1,0:T(8,128)(2,1)S(1)}, bf16[32,3584]{1,0:T(8,128)(2,1)}, u32[]{:S(2)}) copy-start(bf16[32,3584]{1,0:T(8,128)(2,1)} %reshape.242.step_hbm) | copy-start | bytes 688132
  13.6 1.0 %copy-start.3 = (bf16[64,3584]{1,0:T(8,128)(2,1)S(1)}, bf16[64,3584]{1,0:T(8,128)(2,1)}, u32[]{:S(2)}) copy-start(bf16[64,3584]{1,0:T(8,128)(2,1)} %prefix_hbm.1) | copy-start | bytes 1376260
  14.6 0.8 %copy-start.4 = (bf16[32,512]{1,0:T(8,128)(2,1)S(1)}, bf16[32,512]{1,0:T(8,128)(2,1)}, u32[]{:S(2)}) copy-start(bf16[32,512]{1,0:T(8,128)(2,1)} %reshape.244.rope_ref) | copy-start | bytes 98308
  15.4 0.8 %copy-start.5 = (f32[64,128]{1,0:T(8,128)S(1)}, f32[64,128]{1,0:T(8,128)}, u32[]{:S(2)}) copy-start(f32[64,128]{1,0:T(8,128)} %get-tuple-element.5.sin_ref) | copy-start | bytes 98308
  16.1 0.8 %copy-start.6 = (f32[64,128]{1,0:T(8,128)S(1)}, f32[64,128]{1,0:T(8,128)}, u32[]{:S(2)}) copy-start(f32[64,128]{1,0:T(8,128)} %get-tuple-element.6.cos_ref) | copy-start | bytes 98308

commit v2 on v0

--- a/solution.py
+++ b/solution.py
@@ -1,9 +1,17 @@
+import functools
+
 import jax
 import jax.numpy as jnp
 from jax import lax
+from jax.experimental import pallas as pl
+from jax.experimental.pallas import tpu as pltpu
 from jax.sharding import PartitionSpec as P
 
 PREFIX = 1024
+MESH = pl.DeviceIdType.MESH
+NEG = -1e30
+LOG2E = 1.4426950408889634
+LOG1E4 = 9.210340371976184
 
 
 def apply_rotary_embedding(values, positions):
@@ -158,6 +166,393 @@
     return projected.reshape(slot_count, step_count, -1).astype(jnp.bfloat16)
 
 
+def rotate(x, cosine, signed_sine):
+    lane = lax.broadcasted_iota(jnp.int32, x.shape, 1) % 64
+    swapped = jnp.where(lane < 32, pltpu.roll(x, 96, 1), pltpu.roll(x, 32, 1))
+    return x * cosine + swapped * signed_sine
+
+
+def fused_kernel(
+    len_ref,
+    count_ref,
+    prefix_hbm,
+    step_hbm,
+    down_hbm,
+    nope_hbm,
+    rope_hbm,
+    absorb_hbm,
+    value_hbm,
+    cache_hbm,
+    gain_hbm,
+    out_ref,
+    hidden,
+    step,
+    down,
+    nope_rows,
+    rope_rows,
+    absorb,
+    value,
+    cache,
+    gain,
+    fresh,
+    keys,
+    queries,
+    partial,
+    arrived,
+    load_sem,
+    pair_send,
+    pair_recv,
+    send_sem,
+    z_recv,
+    x_recv,
+    y_recv,
+    d1_recv,
+    d2_recv,
+    s_recv,
+    *,
+    chunks,
+    logit_scale,
+):
+    dp = lax.axis_index("dp")
+    tp = lax.axis_index("tp")
+    z, y, x = dp // 4, (dp // 2) % 2, dp % 2
+    latent = gain.shape[1]
+    width = keys.shape[1]
+    heads, nope, _ = absorb.shape
+    slots, _, ctx = cache.shape
+    share = 32
+    rows = 32
+    f32, bf = jnp.float32, jnp.bfloat16
+
+    def place(zz, yy, xx):
+        return zz * 4 + yy * 2 + xx
+
+    x_dev = (place(z, y, 1 - x), tp)
+    y_dev = (place(z, 1 - y, x), tp)
+    sib_dev = (dp, 1 - tp)
+    z_devs = {d: (place(lax.rem(z + d, 4), y, x), tp) for d in (1, 2, 3)}
+
+    barrier = pltpu.get_barrier_semaphore()
+    for dev in (x_dev, y_dev, sib_dev, z_devs[1], z_devs[2], z_devs[3]):
+        pl.semaphore_signal(barrier, inc=1, device_id=dev, device_id_type=MESH)
+
+    prefix_rows, model = prefix_hbm.shape
+    depth = model // chunks
+
+    def load(src, dst, i):
+        copy = pltpu.make_async_copy(src, dst, load_sem.at[i])
+        copy.start()
+        return copy
+
+    step_load = load(step_hbm, step, 0)
+    prefix_load = load(prefix_hbm, hidden.at[pl.ds(0, prefix_rows), :], 1)
+    down_loads = []
+    for i in range(chunks):
+        span = pl.ds(i * depth, depth)
+        down_loads.append(load(down_hbm.at[:, span], down.at[:, span], 8 + i))
+    nope_load = load(nope_hbm, nope_rows, 2)
+    rope_load = load(rope_hbm, rope_rows, 3)
+    absorb_load = load(absorb_hbm, absorb, 4)
+    gain_load = load(gain_hbm, gain, 5)
+    cache_load = load(cache_hbm, cache, 6)
+    value_load = load(value_hbm, value, 7)
+
+    def padded(value_rows):
+        wide = value_rows.astype(f32)
+        return jnp.concatenate([wide, jnp.zeros((rows - wide.shape[0], wide.shape[1]), f32)], axis=0)
+
+    sub = lax.broadcasted_iota(jnp.int32, (8, 128), 0)
+    lane = lax.broadcasted_iota(jnp.int32, (8, 128), 1)
+    lens = jnp.zeros((8, 128), jnp.int32)
+    for s in range(slots):
+        lens = jnp.where(sub == s, len_ref[s], lens)
+    half = (width - latent) // 2
+    frequency = jnp.exp((lane % half).astype(f32) * (-LOG1E4 / half))
+    first = dp * prefix_rows + tp * share
+    sign = jnp.where(lane % (2 * half) < half, -1.0, 1.0)
+    cosines, sines = [], []
+    for g in range((share + rows) // 8):
+        if g < share // 8:
+            position = first + g * 8 + sub
+        else:
+            position = PREFIX + lens + (g - share // 8)
+        angle = position.astype(f32) * frequency
+        cosines.append(jnp.cos(angle))
+        sines.append(jnp.sin(angle) * sign)
+    key_cos = jnp.concatenate(cosines[: share // 8], axis=0)
+    key_sin = jnp.concatenate(sines[: share // 8], axis=0)
+    step_cos = jnp.concatenate(cosines[share // 8 :], axis=0)
+    step_sin = jnp.concatenate(sines[share // 8 :], axis=0)
+
+    nt = (((1,), (1,)), ((), ()))
+    step_load.wait()
+    hidden[prefix_rows:, :] = padded(step[...]).astype(bf)
+    prefix_load.wait()
+    total = None
+    for i in range(chunks):
+        down_loads[i].wait()
+        part = lax.dot_general(
+            hidden[:, i * depth : (i + 1) * depth],
+            down[:, i * depth : (i + 1) * depth],
+            nt,
+            preferred_element_type=f32,
+        )
+        total = part if total is None else total + part
+    partial[...] = total
+
+    pl.semaphore_wait(barrier, 6)
+    theirs = pl.ds(pl.multiple_of((1 - tp) * share, share), share)
+    mine = pl.ds(pl.multiple_of(tp * share, share), share)
+
+    def remote(src, dst, ssem, rsem, dev):
+        return pltpu.make_async_remote_copy(
+            src_ref=src, dst_ref=dst, send_sem=ssem, recv_sem=rsem, device_id=dev, device_id_type=MESH
+        )
+
+    pair_a = remote(
+        partial.at[theirs, :], arrived.at[pl.ds(0, share), :], pair_send.at[0], pair_recv.at[0], sib_dev
+    )
+    pair_b = remote(
+        partial.at[pl.ds(prefix_rows, rows), :],
+        arrived.at[pl.ds(share, rows), :],
+        pair_send.at[1],
+        pair_recv.at[1],
+        sib_dev,
+    )
+    pair_a.start()
+    pair_b.start()
+
+    nope_load.wait()
+    absorb_load.wait()
+    nopes = padded(nope_rows[...]).astype(bf)
+    for h in range(heads):
+        ql = jnp.dot(nopes[:, h * nope : (h + 1) * nope], absorb[h], preferred_element_type=f32)
+        queries[h * rows : (h + 1) * rows, :latent] = ql.astype(bf)
+    rope_load.wait()
+    ropes = padded(rope_rows[...])
+    for p in range(heads // 2):
+        turned = rotate(ropes[:, p * 128 : (p + 1) * 128], step_cos, step_sin).astype(bf)
+        queries[2 * p * rows : (2 * p + 1) * rows, latent:] = turned[:, :64]
+        queries[(2 * p + 1) * rows : (2 * p + 2) * rows, latent:] = turned[:, 64:]
+    gain_load.wait()
+
+    def finished(raw, cosine, signed_sine):
+        low = raw[:, :latent]
+        factor = lax.rsqrt(jnp.mean(low * low, axis=1, keepdims=True) + 1e-06)
+        rope = raw[:, latent:]
+        turned = rotate(jnp.concatenate([rope, rope], axis=1), cosine, signed_sine)
+        return (low * factor * gain[...]).astype(bf), turned[:, : width - latent].astype(bf)
+
+    pair_a.wait_recv()
+    low, high = finished(partial[mine, :] + arrived[0:share, :], key_cos, key_sin)
+
+    def block(group, d):
+        return (group * 4 + d) * share
+
+    keys[0:share, :latent] = low
+    keys[0:share, latent:] = high
+
+    sends = []
+
+    def send(source, target, size, rsem, dev):
+        copy = remote(
+            keys.at[pl.ds(source, size), :],
+            keys.at[pl.ds(target, size), :],
+            send_sem.at[len(sends)],
+            rsem,
+            dev,
+        )
+        copy.start()
+        sends.append(copy)
+
+    def await_block(start, size, rsem, dev):
+        ref = keys.at[pl.ds(start, size), :]
+        remote(ref, ref, send_sem.at[0], rsem, dev).wait_recv()
+
+    def along(d):
+        source = block(0, d)
+        send(source, block(2, d), share, x_recv.at[d], x_dev)
+        send(source, block(3, d), share, y_recv.at[d], y_dev)
+        send(source, block(1, d), share, s_recv.at[d], sib_dev)
+
+    for d in (2, 1, 3):
+        send(0, block(0, d), share, z_recv.at[d], z_devs[d])
+    along(0)
+
+    pair_b.wait_recv()
+    low, high = finished(partial[prefix_rows:, :] + arrived[share:, :], step_cos, step_sin)
+    fresh[0:rows, :latent] = low
+    fresh[0:rows, latent:] = high
+    fresh[rows:, :] = jnp.zeros((fresh.shape[0] - rows, width), bf)
+
+    for d in (1, 3, 2):
+        await_block(block(0, d), share, z_recv.at[d], z_devs[d])
+        along(d)
+
+    cache_load.wait()
+    q = queries[...]
+    factor = logit_scale * LOG2E
+
+    def own_scores(s):
+        raw = jnp.dot(q, cache[s], preferred_element_type=f32).reshape(heads * rows // 8, 8, ctx)
+        valid = (sub == s) & (lane < len_ref[s])
+        return jnp.where(valid[None], raw, NEG).reshape(heads * rows, ctx)
+
+    parts = [own_scores(s) for s in range(slots)]
+    r32 = lax.broadcasted_iota(jnp.int32, (rows, 128), 0)
+    c32 = lax.broadcasted_iota(jnp.int32, (rows, 128), 1)
+    ok = (c32 % 8 == r32 % 8) & (c32 // 8 <= r32 // 8)
+    raw = lax.dot_general(q, fresh[...], nt, preferred_element_type=f32).reshape(heads, rows, 128)
+    parts.append(jnp.where(ok[None], raw, NEG).reshape(heads * rows, 128))
+
+    def forward(d):
+        source = block(2, d)
+        await_block(source, share, x_recv.at[d], x_dev)
+        send(source, block(6, d), share // 2, d1_recv.at[d], y_dev)
+        send(source, block(4, d), share, s_recv.at[4 + d], sib_dev)
+        source = block(3, d)
+        await_block(source, share, y_recv.at[d], y_dev)
+        send(source + share // 2, block(6, d) + share // 2, share // 2, d2_recv.at[d], x_dev)
+        send(source, block(5, d), share, s_recv.at[8 + d], sib_dev)
+
+    for d in (0, 1, 3, 2):
+        forward(d)
+
+    top = functools.reduce(jnp.maximum, parts)
+    top = jnp.max(top, axis=1, keepdims=True)
+    mass, mixed = None, None
+    weights = [jnp.exp2((part - top) * factor) for part in parts]
+    mass = jnp.sum(functools.reduce(jnp.add, weights), axis=1, keepdims=True)
+    mixed = jnp.dot(weights[slots].astype(bf), fresh[:, :latent], preferred_element_type=f32)
+    for s in range(slots):
+        mixed += lax.dot_general(
+            weights[s].astype(bf), cache[s, :latent, :], nt, preferred_element_type=f32
+        )
+
+    def absorb_keys(start, size, top, mass, mixed):
+        scores = lax.dot_general(q, keys[start : start + size, :], nt, preferred_element_type=f32)
+        higher = jnp.maximum(top, jnp.max(scores, axis=1, keepdims=True))
+        weights = jnp.exp2((scores - higher) * factor)
+        shrink = jnp.exp2((top - higher) * factor)
+        mass = mass * shrink + jnp.sum(weights, axis=1, keepdims=True)
+        mixed = mixed * shrink + jnp.dot(
+            weights.astype(bf), keys[start : start + size, :latent], preferred_element_type=f32
+        )
+        return higher, mass, mixed
+
+    for d in (0, 1, 3, 2):
+        start = block(6, d)
+        await_block(start, share // 2, d1_recv.at[d], y_dev)
+        await_block(start + share // 2, share // 2, d2_recv.at[d], x_dev)
+        send(start, block(7, d), share, s_recv.at[12 + d], sib_dev)
+    for d in range(4):
+        await_block(block(1, d), share, s_recv.at[d], sib_dev)
+    top, mass, mixed = absorb_keys(0, 16 * share, top, mass, mixed)
+
+    for group, at in ((4, 4), (5, 8), (7, 12)):
+        for d in range(4):
+            await_block(block(group, d), share, s_recv.at[at + d], sib_dev)
+    top, mass, mixed = absorb_keys(16 * share, 16 * share, top, mass, mixed)
+
+    mixed = (mixed / mass).astype(bf)
+    value_load.wait()
+    vdim = value.shape[2]
+    live = out_ref.shape[0]
+    alive = lax.broadcasted_iota(jnp.int32, (live, vdim), 0) % 8 < count_ref[0]
+    for h in range(heads):
+        up = jnp.dot(mixed[h * rows : (h + 1) * rows, :], value[h], preferred_element_type=f32)
+        out_ref[:, h * vdim : (h + 1) * vdim] = jnp.where(alive, up[:live], 0.0).astype(bf)
+
+    pair_a.wait_send()
+    pair_b.wait_send()
+    for copy in sends:
+        copy.wait_send()
+
+
+def local_fused(
+    prefix_hidden,
+    down_kv,
+    latent_gain,
+    step_hidden,
+    query_nope,
+    query_rope,
+    key_absorb,
+    value_up,
+    cache,
+    cache_len,
+    counts,
+):
+    key_width = down_kv.shape[1]
+    latent_width = latent_gain.shape[0]
+    slots, steps, _ = step_hidden.shape
+    heads, nope_width, _ = key_absorb.shape
+    vdim = value_up.shape[2]
+    logit_scale = (nope_width + key_width - latent_width) ** (-0.5)
+    block_rows, model = prefix_hidden.shape
+    share = block_rows // 2
+    rows = 32
+
+    def by_step(values):
+        return values.transpose(1, 0, 2).reshape(steps * slots, -1)
+
+    chunks = 7
+    vmem = pl.BlockSpec(memory_space=pltpu.VMEM)
+    smem = pl.BlockSpec(memory_space=pltpu.SMEM)
+    hbm = pl.BlockSpec(memory_space=pltpu.HBM)
+    dma = pltpu.SemaphoreType.DMA
+    bf, f32 = jnp.bfloat16, jnp.float32
+    operands = (
+        cache_len,
+        counts,
+        prefix_hidden,
+        by_step(step_hidden),
+        down_kv.T,
+        by_step(query_nope),
+        by_step(query_rope),
+        key_absorb,
+        value_up,
+        cache.transpose(0, 2, 1),
+        latent_gain[None, :],
+    )
+    step_in, down_in, nope_in, rope_in = operands[3:7]
+    out = pl.pallas_call(
+        functools.partial(fused_kernel, chunks=chunks, logit_scale=logit_scale),
+        out_shape=jax.ShapeDtypeStruct((steps * slots, heads * vdim), bf),
+        in_specs=[smem, smem] + [hbm] * 9,
+        out_specs=vmem,
+        scratch_shapes=[
+            pltpu.VMEM((block_rows + rows, model), bf),
+            pltpu.VMEM(step_in.shape, bf),
+            pltpu.VMEM(down_in.shape, bf),
+            pltpu.VMEM(nope_in.shape, bf),
+            pltpu.VMEM(rope_in.shape, bf),
+            pltpu.VMEM(key_absorb.shape, bf),
+            pltpu.VMEM(value_up.shape, bf),
+            pltpu.VMEM(operands[9].shape, bf),
+            pltpu.VMEM((1, latent_width), f32),
+            pltpu.VMEM((128, key_width), bf),
+            pltpu.VMEM((PREFIX, key_width), bf),
+            pltpu.VMEM((heads * rows, key_width), bf),
+            pltpu.VMEM((block_rows + rows, key_width), f32),
+            pltpu.VMEM((share + rows, key_width), f32),
+            dma((8 + chunks,)),
+            dma((2,)),
+            dma((2,)),
+            dma((35,)),
+            dma((4,)),
+            dma((4,)),
+            dma((4,)),
+            dma((4,)),
+            dma((4,)),
+            dma((16,)),
+        ],
+        compiler_params=pltpu.CompilerParams(
+            collective_id=0, has_side_effects=True, vmem_limit_bytes=62 * 1024 * 1024
+        ),
+    )(*operands)
+    return out.reshape(steps, slots, heads * vdim).transpose(1, 0, 2)
+
+
 def solution(mesh):
     in_specs = (
         P("dp", "tp"),
@@ -173,4 +568,5 @@
         P("dp"),
     )
     out_specs = P("dp", None, "tp")
-    return jax.shard_map(local, mesh=mesh, in_specs=in_specs, out_specs=out_specs, check_vma=False)
+    fused = mesh.shape["dp"] == 16 and mesh.shape["tp"] == 2
+    return jax.shard_map(local_fused if fused else local, mesh=mesh, in_specs=in_specs, out_specs=out_specs, check_vma=False)

time: 94.7 us -> 27.9 us (0.29)
  waiting for transfers between devices: 51.2 us -> 0 us
  Pallas kernels: 0 us -> 25.4 us
  matrix products: 14.4 us -> 0 us
  between operations: 14.4 us -> 0.66 us
  other arithmetic: 5.73 us -> 0 us
  blocking collectives: 3.58 us -> 0 us
  local copies, waits for them, and re-layouts: 4.68 us -> 1.42 us
    all_gather x1 -> x0, waiting for transfers between devices: 49.4 us -> none  [local(): key_piece = lax.all_gather(prefix_keys, ('dp', 'tp'), axis=0, tiled=True)]
    pallas_call x0 -> x1, Pallas kernels: none -> 25.4 us  [local_fused(): pl.pallas_call(functools.partial(fused_kernel, chunks=chunks, logit_scale...]
    dot_general x8 -> x0, matrix products: 14.4 us -> none  [the longest x1 4.39 us: local(): jnp.dot(prefix_hidden, down_kv, preferred_element_type=jnp.float32)]
    psum x1 -> x0, blocking collectives: 3.58 us -> none  [local(): lax.psum(step_part, 'tp').reshape(slot_count, step_count, key_width)]
    reduce_sum x4 -> x0, other arithmetic: 2.54 us -> none  [the longest x1 1.21 us: own_keys(): row_mass = row_mass * shrink + jnp.sum(weights, axis=2, keepdims=True)]
    another operation x5 -> x0, other arithmetic: 1.98 us -> none
    reduce_scatter x1 -> x0, waiting for transfers between devices: 1.8 us -> none  [local(): lax.psum_scatter(partial_rows, 'tp', scatter_dimension=0, tiled=True)]
    concatenate x2 -> x0, local copies, waits for them, and re-layouts: 1.36 us -> none  [the longest x1 0.72 us: local(): jnp.concatenate([query_latent, query_rot], axis=-1)]
  transfers between devices with their start and end apart: 2 -> 0, of which waited for: 2 -> 0; matrix products, arithmetic and copies ran while one was open for 10% -> 0% of each run, Pallas kernels for 0% -> 0%
where the time goes in v2:
time: 27.9 us; the launch traced here: 27.4 us
  Pallas kernels  25.4 us (91%)
  local copies, waits for them, and re-layouts  1.42 us (5%)
  between operations  0.66 us (2%)
    pallas_call x1, Pallas kernels, local_fused(): pl.pallas_call(functools.partial(fused_kernel, chunks=chunks, logit_scale...  25.4 us
    unnamed x1, local copies, waits for them, and re-layouts  1.42 us

profile of v2, /device:TPU:1, one launch (start us, length us, event | category | flops | bytes accessed | tf_op | source)
XLA Modules:
  0.0 27.4 jit_solution(771197138882931493)
XLA Ops:
  0.7 25.4 %shard_map.109 = bf16[24,1024]{1,0:T(8,128)(2,1)} custom-call(s32[8]{0:T(128)} %len_ref.1, s32[1]{0:T(128)S(6)} %copy.13.count_ref, bf16[64,3584]{1,0:T(8,128)(2,1)} %prefix_hbm.1, bf16[24,3584]{1,0:T(8,128)(2,1)} %bitcast.18, bf16[576,3584]{1,0:T(8,128)(2,1)} %bitcast.15, bf16[24,1024]{1,0:T(8,128)(2,1)} %bitcast.19, bf16[24,512]{1,0:T(8,128)(2,1)} %bitcast.20, ...), custom_call_target="tpu_custom_call" | custom-call | tf_op jit(solution)/shard_map/pallas_call | solution.py:518
  26.0 1.4 %copy.14 = bf16[8,3,1024]{2,0,1:T(8,128)(2,1)} copy(bf16[8,3,1024]{2,0,1:T(8,128)(2,1)} %bitcast.17) | data formatting | bytes 98304

commit v3 on v2

--- a/solution.py
+++ b/solution.py
@@ -206,8 +206,7 @@
     z_recv,
     x_recv,
     y_recv,
-    d1_recv,
-    d2_recv,
+    d_recv,
     s_recv,
     *,
     chunks,
@@ -229,11 +228,16 @@
 
     x_dev = (place(z, y, 1 - x), tp)
     y_dev = (place(z, 1 - y, x), tp)
+    xy_dev = (place(z, 1 - y, 1 - x), tp)
     sib_dev = (dp, 1 - tp)
     z_devs = {d: (place(lax.rem(z + d, 4), y, x), tp) for d in (1, 2, 3)}
 
+    first_d = jnp.where(z == 0, 3, 1)
+    second_d = jnp.where((z == 0) | (z == 3), 2, 3)
+    third_d = jnp.where(z == 0, 1, jnp.where(z == 3, 3, 2))
+    others = (first_d, second_d, third_d)
     barrier = pltpu.get_barrier_semaphore()
-    for dev in (x_dev, y_dev, sib_dev, z_devs[1], z_devs[2], z_devs[3]):
+    for dev in (x_dev, y_dev, xy_dev, sib_dev, z_devs[1], z_devs[2], z_devs[3]):
         pl.semaphore_signal(barrier, inc=1, device_id=dev, device_id_type=MESH)
 
     prefix_rows, model = prefix_hbm.shape
@@ -300,7 +304,7 @@
         total = part if total is None else total + part
     partial[...] = total
 
-    pl.semaphore_wait(barrier, 6)
+    pl.semaphore_wait(barrier, 7)
     theirs = pl.ds(pl.multiple_of((1 - tp) * share, share), share)
     mine = pl.ds(pl.multiple_of(tp * share, share), share)
 
@@ -347,7 +351,8 @@
     low, high = finished(partial[mine, :] + arrived[0:share, :], key_cos, key_sin)
 
     def block(group, d):
-        return (group * 4 + d) * share
+        at = (group * 4 + d) * share
+        return at if isinstance(d, int) else pl.multiple_of(at, share)
 
     keys[0:share, :latent] = low
     keys[0:share, latent:] = high
@@ -371,6 +376,7 @@
 
     def along(d):
         source = block(0, d)
+        send(source, block(6, d), share, d_recv.at[d], xy_dev)
         send(source, block(2, d), share, x_recv.at[d], x_dev)
         send(source, block(3, d), share, y_recv.at[d], y_dev)
         send(source, block(1, d), share, s_recv.at[d], sib_dev)
@@ -385,8 +391,8 @@
     fresh[0:rows, latent:] = high
     fresh[rows:, :] = jnp.zeros((fresh.shape[0] - rows, width), bf)
 
-    for d in (1, 3, 2):
-        await_block(block(0, d), share, z_recv.at[d], z_devs[d])
+    for d in others:
+        await_block(block(0, d), share, z_recv.at[d], z_devs[1])
         along(d)
 
     cache_load.wait()
@@ -408,14 +414,12 @@
     def forward(d):
         source = block(2, d)
         await_block(source, share, x_recv.at[d], x_dev)
-        send(source, block(6, d), share // 2, d1_recv.at[d], y_dev)
         send(source, block(4, d), share, s_recv.at[4 + d], sib_dev)
         source = block(3, d)
         await_block(source, share, y_recv.at[d], y_dev)
-        send(source + share // 2, block(6, d) + share // 2, share // 2, d2_recv.at[d], x_dev)
         send(source, block(5, d), share, s_recv.at[8 + d], sib_dev)
 
-    for d in (0, 1, 3, 2):
+    for d in (0, *others):
         forward(d)
 
     top = functools.reduce(jnp.maximum, parts)
@@ -440,10 +444,9 @@
         )
         return higher, mass, mixed
 
-    for d in (0, 1, 3, 2):
+    for d in (0, *others):
         start = block(6, d)
-        await_block(start, share // 2, d1_recv.at[d], y_dev)
-        await_block(start + share // 2, share // 2, d2_recv.at[d], x_dev)
+        await_block(start, share, d_recv.at[d], xy_dev)
         send(start, block(7, d), share, s_recv.at[12 + d], sib_dev)
     for d in range(4):
         await_block(block(1, d), share, s_recv.at[d], sib_dev)
@@ -538,8 +541,7 @@
             dma((8 + chunks,)),
             dma((2,)),
             dma((2,)),
-            dma((35,)),
-            dma((4,)),
+            dma((31,)),
             dma((4,)),
             dma((4,)),
             dma((4,)),

time: 27.9 us -> 25.7 us (0.921)
  the two profiles are of different devices: /device:TPU:1 before, /device:TPU:17 now
where the time goes in v3:
time: 25.7 us; the launch traced here: 25.5 us
  Pallas kernels  23.5 us (91%)
  local copies, waits for them, and re-layouts  1.42 us (6%)
  between operations  0.66 us (3%)
    pallas_call x1, Pallas kernels, local_fused(): pl.pallas_call(functools.partial(fused_kernel, chunks=chunks, logit_scale...  23.5 us
    unnamed x1, local copies, waits for them, and re-layouts  1.42 us

profile of v3, /device:TPU:17, one launch (start us, length us, event | category | flops | bytes accessed | tf_op | source)
XLA Modules:
  0.0 25.5 jit_solution(15353026023747804131)
XLA Ops:
  0.7 23.5 %shard_map.109 = bf16[24,1024]{1,0:T(8,128)(2,1)} custom-call(s32[8]{0:T(128)} %len_ref.1, s32[1]{0:T(128)S(6)} %copy.13.count_ref, bf16[64,3584]{1,0:T(8,128)(2,1)} %prefix_hbm.1, bf16[24,3584]{1,0:T(8,128)(2,1)} %bitcast.18, bf16[576,3584]{1,0:T(8,128)(2,1)} %bitcast.15, bf16[24,1024]{1,0:T(8,128)(2,1)} %bitcast.19, bf16[24,512]{1,0:T(8,128)(2,1)} %bitcast.20, ...), custom_call_target="tpu_custom_call" | custom-call | tf_op jit(solution)/shard_map/pallas_call | solution.py:521
  24.1 1.4 %copy.14 = bf16[8,3,1024]{2,0,1:T(8,128)(2,1)} copy(bf16[8,3,1024]{2,0,1:T(8,128)(2,1)} %bitcast.17) | data formatting | bytes 98304
